TPU v7x, 256 devices: a whole 4x4x8 slice. The times are simulated.
256 devices in a mesh: pair: 16 (over x, z_lo), tp: 8 (over y, z_hi), rep: 2 (over core).
Axes of the slice: x: 4, y: 4, z: 8 (z_hi: 2, z_lo: 4; z = z_hi * 4 + z_lo), core: 2. Of those that a mesh axis runs over, the one named last changes fastest.
Arguments:
- normed: bfloat16 [2, 16, 8192], P(None, 'rep', 'pair'), parts along dimension 1, may hold values from -6 to 6
- w_query: bfloat16 [8192, 8192], P('pair', 'tp'), may hold values from -0.0625 to 0.0625
- b_query: float32 [8192], P('tp'), may hold values from -3 to 3
- w_key: bfloat16 [8192, 1024], P('pair', 'tp'), may hold values from -0.25 to 0.25
- b_key: float32 [1024], P('tp'), may hold values from -8 to 8
- w_value: bfloat16 [8192, 1024], P('pair', 'tp'), may hold values from -0.0625 to 0.0625
- b_value: float32 [1024], P('tp'), may hold values from -5 to 5
- w_out: bfloat16 [8192, 8192], P('tp', 'pair'), may hold values from -0.5 to 0.5
- pool: bfloat16 [32, 8, 512, 16, 256], P(('rep', 'pair'), 'tp'), parts along dimension 0, as said below
- page_table: int32 [32, 512], P(('rep', 'pair')), parts along dimension 0, may hold values from 0 to 511, as said below
- lengths: int32 [16], P('rep'), parts along dimension 0, may hold values from 8192 to 12286, as said below
- plan: int32 [16, 2], P('rep'), parts along dimension 0, may hold values from 0 to 64, as said below
Outputs:
- attended: float32 [2, 16, 8192], P(None, 'rep', 'pair'), parts along dimension 1
- new_pool: bfloat16 [32, 8, 512, 16, 256], P(('rep', 'pair'), 'tp'), parts along dimension 0
There are 2 independent parts, one for each index of `rep`. A program takes and returns all parts, laid end to end along the dimension named above; an argument that names none is the same for every part. Nothing has to cross between parts.
Inputs may be any that keep to these rules, and one draw needn't show every extreme that they name: `pool`: cached keys (first 128 entries of a slot row, already rotated) and values. `page_table`: each row is an order of the 512 slots of one pool. `lengths`: some request reaches the most. `plan`: some entry reaches the most.
All inputs are finite; a program needn't handle non-finite values.
Results may differ from a plain program's by a relative error of at most 0.011.
The roundings to bfloat16 on the way count: a program that leaves them out, or rounds other values in their place, can miss the bound.
Values may be sent and summed in bfloat16 or wider, within the bound.
A program may use at most 64 MiB of HBM per device.

v0:
```python
import math

import jax
import jax.numpy as jnp
from jax import lax
from jax.sharding import PartitionSpec as P

PAGES_HALF = 384
STEPS = 2
SECTION = 64


rope_base = 1000000.0


def from_behind(block, axis, distance):
    devices = range(lax.axis_size(axis))
    route = [(i - distance, i) for i in devices if i - distance in devices]
    return lax.ppermute(block, axis, route)


def from_behind_2(block, axis, distance):
    devices = range(lax.axis_size(axis))
    route = [((i - distance) % len(devices), i) for i in devices]
    return lax.ppermute(block, axis, route)


def rotate(vectors, position):
    half_size = vectors.shape[-1] // 2
    frequency = rope_base ** (-(jnp.arange(half_size, dtype=jnp.float32) * 2.0 / vectors.shape[-1]))
    angles = position * frequency
    cosine = jnp.cos(angles)
    sine_val = jnp.sin(angles)
    first_half = vectors[..., :half_size]
    second_half = vectors[..., half_size:]
    return jnp.concatenate(
        [
            first_half * cosine - second_half * sine_val,
            second_half * cosine + first_half * sine_val,
        ],
        -1,
    )


def merge_halves(first_max, first_sum, first_out, second_max, second_sum, second_out):
    joint_max = jnp.maximum(first_max, second_max)
    left_weight = jnp.exp(first_max - joint_max)
    right_weight = jnp.exp(second_max - joint_max)
    joined = left_weight[..., None] * first_out + right_weight[..., None] * second_out
    return joined / (left_weight * first_sum + right_weight * second_sum)[..., None]


def local(
    normed, w_query, b_query, w_key, b_key, w_value, b_value, w_out, pool, page_table, lengths, plan
):
    pair_count = lax.axis_size("pair")
    requests = pair_count // 2
    pair_index = lax.axis_index("pair")
    request_index = pair_index % requests
    source = pair_index >= requests
    head_size = w_key.shape[1]
    group_size = w_query.shape[1] // head_size
    kv_store = pool[0, 0]
    slot_table = page_table[0]
    slot_count = kv_store.shape[0]
    page_len = kv_store.shape[1]
    half_pages = PAGES_HALF
    section_pages = SECTION
    half_tokens = half_pages * page_len
    picker = jnp.arange(requests, dtype=jnp.int32) == request_index
    length = jnp.sum(jnp.where(picker, lengths, 0))
    sched_row = jnp.sum(jnp.where(picker[:, None], plan, 0), 0)
    slot_ids = jnp.arange(slot_count, dtype=jnp.int32)
    inverse = jnp.sum(jnp.where(slot_table[:, None] == slot_ids[None, :], slot_ids[:, None], 0), 0)
    logical = jnp.broadcast_to(inverse[:, None], (slot_count, page_len)).reshape(-1)
    token_offset = (
        inverse[:, None] * page_len + jnp.arange(page_len, dtype=jnp.int32)[None, :]
    ).reshape(-1)
    score_scale = 1.0 / math.sqrt(head_size)
    anchor = jnp.int32(0)
    row_width = group_size * head_size
    half_width = row_width // 2
    moved_total = jnp.int32(0)
    results = []
    for step_index in range(STEPS):
        hidden = normed[step_index]
        summed = lax.psum(
            (
                jnp.dot(hidden, w_query, preferred_element_type=jnp.float32),
                jnp.dot(hidden, w_key, preferred_element_type=jnp.float32),
                jnp.dot(hidden, w_value, preferred_element_type=jnp.float32),
            ),
            "pair",
        )
        query_row = jnp.sum(jnp.where(picker[:, None], summed[0], 0.0), 0) + b_query
        key_row = jnp.sum(jnp.where(picker[:, None], summed[1], 0.0), 0) + b_key
        value_row = jnp.sum(jnp.where(picker[:, None], summed[2], 0.0), 0) + b_value
        position = (length + step_index).astype(jnp.float32)
        query_rot = rotate(query_row.reshape(group_size, head_size), position).astype(jnp.bfloat16)
        key_rot = rotate(key_row, position).astype(jnp.bfloat16)
        value_new = value_row.astype(jnp.bfloat16)
        offset = length - half_tokens + step_index
        write_slot = slot_table[offset // page_len]
        write_row = offset % page_len
        new_entry = jnp.concatenate([key_rot, value_new])[None, None, :]
        old_entry = lax.dynamic_slice(
            kv_store, (write_slot, write_row, anchor), (1, 1, 2 * head_size)
        )
        kv_store = lax.dynamic_update_slice(
            kv_store, jnp.where(source, new_entry, old_entry), (write_slot, write_row, anchor)
        )
        moved_now = sched_row[step_index]
        page_picks = moved_total + jnp.arange(section_pages, dtype=jnp.int32)
        outgoing = kv_store[slot_table[page_picks]]
        incoming = from_behind(outgoing, "pair", -requests)
        targets = slot_table[half_pages + page_picks]
        keep_mask = (jnp.arange(section_pages, dtype=jnp.int32) < moved_now) & jnp.logical_not(
            source
        )
        kv_store = kv_store.at[targets].set(
            jnp.where(keep_mask[:, None, None], incoming, kv_store[targets])
        )
        moved_total = moved_total + moved_now
        handed = 0
        live_source = (logical < half_pages) & (logical >= handed) & (token_offset <= offset)
        live_target = logical < half_pages + handed
        visible = jnp.where(source, live_source, live_target)
        key_rows = kv_store[:, :, :head_size].reshape(-1, head_size)
        value_rows = kv_store[:, :, head_size:].reshape(-1, head_size)
        scores = (
            jnp.einsum("gd,td->gt", query_rot, key_rows, preferred_element_type=jnp.float32)
            * score_scale
        )
        scores = jnp.where(visible[None, :], scores, -1e30)
        row_max = jnp.max(scores, 1)
        weights = jnp.where(visible[None, :], jnp.exp(scores - row_max[:, None]), 0.0)
        row_sum = jnp.sum(weights, 1)
        head_out = jnp.dot(
            weights.astype(jnp.bfloat16), value_rows, preferred_element_type=jnp.float32
        )
        other_max, other_sum, other_out = from_behind_2(
            (row_max, row_sum, head_out), "pair", requests
        )
        merged = merge_halves(row_max, row_sum, head_out, other_max, other_sum, other_out)
        flat_row = merged.astype(jnp.bfloat16).reshape(row_width)
        own_piece = jnp.where(source, flat_row[half_width:], flat_row[:half_width])[None]
        gathered = lax.all_gather(own_piece, "pair", axis=0, tiled=True)
        attended_rows = jnp.concatenate([gathered[:requests], gathered[requests:]], 1)
        projected = jnp.dot(attended_rows, w_out, preferred_element_type=jnp.float32)
        results.append(lax.psum(projected, "tp"))
    return (jnp.stack(results), kv_store[None, None])


def solution(mesh):
    return jax.shard_map(
        local,
        mesh=mesh,
        in_specs=(
            P(None, "rep", "pair"),
            P("pair", "tp"),
            P("tp"),
            P("pair", "tp"),
            P("tp"),
            P("pair", "tp"),
            P("tp"),
            P("tp", "pair"),
            P(("rep", "pair"), "tp", None, None, None),
            P(("rep", "pair"), None),
            P("rep"),
            P("rep", None),
        ),
        out_specs=(P(None, "rep", "pair"), P(("rep", "pair"), "tp", None, None, None)),
        check_vma=False,
    )
```

profile of v0, /device:TPU:8, one launch (start us, length us, event | category | flops | bytes accessed | tf_op | source)
XLA Modules:
  0.0 371.1 jit_solution(16909548559511858322)
XLA Ops:
  7.2 4.5 %copy.49 = bf16[1,1,512,16,256]{4,3,2,1,0:T(8,128)(2,1)} copy(bf16[1,1,512,16,256]{4,3,2,1,0:T(8,128)(2,1)} %param.20) | data formatting | bytes 8388608
  11.8 0.8 fusion.28
  12.7 0.9 fusion.34
  23.5 0.8 gather_fusion.1
  24.3 0.8 gather_fusion
  28.2 0.8 gather_fusion.5
  29.0 0.8 gather_fusion.4
  31.9 137.4 %all-reduce.4.cloned.1.call-done = (f32[8,128]{1,0:T(8,128)}, f32[8,128]{1,0:T(8,128)}, f32[8,128]{1,0:T(8,128)}, f32[8,128]{1,0:T(8,128)}, f32[8,1024]{1,0:T(8,128)}, /*index=5*/f32[8,1024]{1,0:T(8,128)}) async-done(((f32[8,128]{1,0:T(8,128)}, f32[8,128]{1,0:T(8,128)}, f32[8,128]{1,0:T(8,128)}, f32[8,128]{1,0:T(8,128)}, f32[8,1024]{1,0:T(8,128)}, /*index=5*/f32[8,1024]{1,0:T(8,128)}), (f32[8,128]{1,0:T(8,128)}, ...) | async-done | bytes 81936 | tf_op jit(solution)/shard_map/psum | solution.py:87
  169.3 0.8 select_reduce_fusion.4
  170.9 1.3 dynamic_update_slice.6
  172.2 2.8 gather_fusion.2
  175.0 1.3 collective-permute-start
  176.3 2.8 gather_fusion.3
  179.5 8.1 %collective-permute-done = bf16[64,16,256]{2,1,0:T(8,128)(2,1)S(1)} collective-permute-done((bf16[64,16,256]{2,1,0:T(8,128)(2,1)S(1)}, bf16[64,16,256]{2,1,0:T(8,128)(2,1)S(1)}, u32[]{:S(2)}, u32[]{:S(2)}) %collective-permute-start) | collective-permute-done | bytes 524320 | tf_op jit(solution)/shard_map/ppermute | solution.py:19
  187.7 7.1 %scatter_fusion = bf16[512,16,256]{2,1,0:T(8,128)(2,1)} fusion(bf16[512,16,256]{2,1,0:T(8,128)(2,1)} %dynamic_update_slice.6, s32[64]{0:T(128)S(1)} %fusion.53, bf16[64,16,256]{2,1,0:T(8,128)(2,1)S(1)} %broadcast_select_fusion.1), kind=kCustom, calls=%fused_computation.8 | custom fusion | bytes 1573120 | tf_op jit(solution)/shard_map/scatter | solution.py:120
  194.9 2.9 fusion.69
  197.8 0.8 fusion.76
  199.0 3.6 collective-permute-start.3
  203.8 1.3 dynamic_update_slice.7
  205.1 2.8 gather_fusion.6
  207.9 1.3 collective-permute-start.4
  209.2 2.8 gather_fusion.7
  212.2 40.8 %all-gather = bf16[16,1,512]{2,1,0:T(2,128)(2,1)S(1)} all-gather(bf16[1,1,512]{2,1,0:T(2,128)(2,1)S(1)} %reshape.402), channel_id=1, replica_groups=mesh['pair'=16,'tp'=8,'rep'=2] {'pair'}, dimensions={0}, use_global_device_ids=true | all-gather | bytes 17408 | tf_op jit(solution)/shard_map/all_gather | solution.py:147
  253.3 1.2 broadcast_select_fusion
  254.5 7.1 %scatter_fusion.1 = bf16[512,16,256]{2,1,0:T(8,128)(2,1)} fusion(bf16[512,16,256]{2,1,0:T(8,128)(2,1)} %dynamic_update_slice.7, s32[64]{0:T(128)S(1)} %fusion.56, bf16[64,16,256]{2,1,0:T(8,128)(2,1)S(1)} %broadcast_select_fusion), kind=kCustom, calls=%fused_computation.9 | custom fusion | bytes 1573120 | tf_op jit(solution)/shard_map/scatter | solution.py:120
  261.6 2.9 fusion.70
  264.6 0.8 fusion.75
  265.7 3.6 collective-permute-start.7
  269.9 1.0 collective-permute-done.7
  270.9 4.1 %collective-permute-done.6 = f32[8,128]{1,0:T(8,128)S(1)} collective-permute-done((f32[8,128]{1,0:T(8,128)S(1)}, f32[8,128]{1,0:T(8,128)S(1)}, u32[]{:S(2)}, u32[]{:S(2)}) %collective-permute-start.6) | collective-permute-done | bytes 4128 | tf_op jit(solution)/shard_map/ppermute | solution.py:25
  275.1 36.9 %all-gather.1 = bf16[16,1,512]{2,1,0:T(2,128)(2,1)S(1)} all-gather(bf16[1,1,512]{2,1,0:T(2,128)(2,1)S(1)} %reshape.404), channel_id=1, replica_groups=mesh['pair'=16,'tp'=8,'rep'=2] {'pair'}, dimensions={0}, use_global_device_ids=true | all-gather | bytes 17408 | tf_op jit(solution)/shard_map/all_gather | solution.py:147
  312.3 51.3 %all-reduce.1 = (f32[1,8,512]{2,1,0:T(8,128)S(1)}, f32[1,8,512]{2,1,0:T(8,128)S(1)}) all-reduce(f32[1,8,512]{2,1,0:T(8,128)S(1)} %convolution_bitcast_fusion, f32[1,8,512]{2,1,0:T(8,128)S(1)} %convolution_bitcast_fusion.1), channel_id=1, replica_groups=mesh['pair'=16,'tp'=8,'rep'=2] {'tp'}, use_global_device_ids=true, to_apply=%region_22.23 | all-reduce | flops 8192 | bytes 65536 | tf_op jit(solution)/shard_map/psum | solution.py:150
  (108 shorter events, 13.7 us)
Async XLA Ops:
  7.2 4.6 %copy-start = (bf16[512,1024]{1,0:T(8,128)(2,1)S(1)}, bf16[512,1024]{1,0:T(8,128)(2,1)}, u32[]{:S(2)}) copy-start(bf16[512,1024]{1,0:T(8,128)(2,1)} %param.13) | copy-start | bytes 3145732
  7.2 4.6 %copy-start.5 = (bf16[2,8,512]{2,1,0:T(8,128)(2,1)S(1)}, bf16[2,8,512]{2,1,0:T(8,128)(2,1)}, u32[]{:S(2)}) copy-start(bf16[2,8,512]{2,1,0:T(8,128)(2,1)} %param.12) | copy-start | bytes 49156
  7.2 162.1 %all-reduce.4.cloned.1.call-start = ((), (), s32[]{:S(2)}) async-start(), calls=%async_computation | async-start | bytes 163840 | tf_op jit(solution)/shard_map/psum | solution.py:87
  11.8 1.8 copy-start.3
  11.8 3.2 copy-start.4
  11.8 4.7 %copy-start.12 = (s32[8]{0:T(128)S(1)}, s32[8]{0:T(128)}, u32[]{:S(2)}) copy-start(s32[8]{0:T(128)} %param.22) | copy-start | bytes 100
  11.8 6.9 %copy-start.1 = (s32[1,512]{1,0:T(1,128)S(1)}, s32[1,512]{1,0:T(1,128)}, u32[]{:S(2)}) copy-start(s32[1,512]{1,0:T(1,128)} %param.21) | copy-start | bytes 6148
  11.8 13.3 %copy-start.9 = (s32[8,2]{0,1:T(2,128)S(1)}, s32[8,2]{0,1:T(2,128)}, u32[]{:S(2)}) copy-start(s32[8,2]{0,1:T(2,128)} %param.23) | copy-start | bytes 196
  13.6 156.5 %copy-start.10 = (f32[128]{0:T(128)S(1)}, f32[128]{0:T(128)}, u32[]{:S(2)}) copy-start(f32[128]{0:T(128)} %param.18) | copy-start | bytes 1540
  13.6 156.5 %copy-start.11 = (f32[128]{0:T(128)S(1)}, f32[128]{0:T(128)}, u32[]{:S(2)}) copy-start(f32[128]{0:T(128)} %param.16) | copy-start | bytes 1540
  25.1 154.2 %copy-start.8 = (f32[1024]{0:T(1024)S(1)}, f32[1024]{0:T(1024)}, u32[]{:S(2)}) copy-start(f32[1024]{0:T(1024)} %param.14) | copy-start | bytes 12292
  169.3 9.9 %copy-start.6 = (f32[8,1024]{1,0:T(8,128)S(1)}, f32[8,1024]{1,0:T(8,128)}, u32[]{:S(2)}) copy-start(f32[8,1024]{1,0:T(8,128)} %get-tuple-element.12) | copy-start | bytes 98308
  169.3 9.9 %copy-start.7 = (f32[8,1024]{1,0:T(8,128)S(1)}, f32[8,1024]{1,0:T(8,128)}, u32[]{:S(2)}) copy-start(f32[8,1024]{1,0:T(8,128)} %get-tuple-element.13) | copy-start | bytes 98308
  175.0 12.6 %collective-permute-start = (bf16[64,16,256]{2,1,0:T(8,128)(2,1)S(1)}, bf16[64,16,256]{2,1,0:T(8,128)(2,1)S(1)}, u32[]{:S(2)}, u32[]{:S(2)}) collective-permute-start(bf16[64,16,256]{2,1,0:T(8,128)(2,1)S(1)} %gather_fusion.2), channel_id=1, source_target_pairs={{128,0},{144,16},{160,32},{176,48},{192,64},{208,80},{224,96},{240... | collective-permute-start | bytes 1572872 | tf_op jit(solution)/shard_map/ppermute | solution.py:19
  198.6 13.4 %collective-permute-start.1 = (f32[8]{0:T(128)S(1)}, f32[8]{0:T(128)S(1)}, u32[]{:S(2)}, u32[]{:S(2)}) collective-permute-start(f32[8]{0:T(128)S(1)} %get-tuple-element.56), channel_id=1, source_target_pairs={{128,0},{144,16},{160,32},{176,48},{192,64},{208,80},{224,96},{240... | collective-permute-start | bytes 104 | tf_op jit(solution)/shard_map/ppermute | solution.py:25
  199.0 13.0 %collective-permute-start.3 = (f32[8]{0:T(128)S(1)}, f32[8]{0:T(128)S(1)}, u32[]{:S(2)}, u32[]{:S(2)}) collective-permute-start(f32[8]{0:T(128)S(1)} %fusion.4), channel_id=1, source_target_pairs={{128,0},{144,16},{160,32},{176,48},{192,64},{208,80},{224,96},{240... | collective-permute-start | bytes 104 | tf_op jit(solution)/shard_map/ppermute | solution.py:25
  202.6 50.4 %copy-start.2 = (bf16[1024,512]{1,0:T(8,128)(2,1)S(1)}, bf16[1024,512]{1,0:T(8,128)(2,1)}, u32[]{:S(2)}) copy-start(bf16[1024,512]{1,0:T(8,128)(2,1)} %param.19) | copy-start | bytes 3145732
  203.0 9.0 %collective-permute-start.2 = (f32[8,128]{1,0:T(8,128)S(1)}, f32[8,128]{1,0:T(8,128)S(1)}, u32[]{:S(2)}, u32[]{:S(2)}) collective-permute-start(f32[8,128]{1,0:T(8,128)S(1)} %fusion.10), channel_id=1, source_target_pairs={{128,0},{144,16},{160,32},{176,48},{192,64},{208,80},{224,96},{240... | collective-permute-start | bytes 12296 | tf_op jit(solution)/shard_map/ppermute | solution.py:25
  207.9 45.4 %collective-permute-start.4 = (bf16[64,16,256]{2,1,0:T(8,128)(2,1)S(1)}, bf16[64,16,256]{2,1,0:T(8,128)(2,1)}, u32[]{:S(2)}, u32[]{:S(2)}) collective-permute-start(bf16[64,16,256]{2,1,0:T(8,128)(2,1)S(1)} %gather_fusion.6), channel_id=1, source_target_pairs={{128,0},{144,16},{160,32},{176,48},{192,64},{208,80},{224,96},{240... | collective-permute-start | bytes 1572872 | tf_op jit(solution)/shard_map/ppermute | solution.py:19
  265.4 5.5 %collective-permute-start.5 = (f32[8]{0:T(128)S(1)}, f32[8]{0:T(128)S(1)}, u32[]{:S(2)}, u32[]{:S(2)}) collective-permute-start(f32[8]{0:T(128)S(1)} %get-tuple-element.54), channel_id=1, source_target_pairs={{128,0},{144,16},{160,32},{176,48},{192,64},{208,80},{224,96},{240... | collective-permute-start | bytes 104 | tf_op jit(solution)/shard_map/ppermute | solution.py:25
  265.7 5.1 %collective-permute-start.7 = (f32[8]{0:T(128)S(1)}, f32[8]{0:T(128)S(1)}, u32[]{:S(2)}, u32[]{:S(2)}) collective-permute-start(f32[8]{0:T(128)S(1)} %fusion.6), channel_id=1, source_target_pairs={{128,0},{144,16},{160,32},{176,48},{192,64},{208,80},{224,96},{240... | collective-permute-start | bytes 104 | tf_op jit(solution)/shard_map/ppermute | solution.py:25
  269.8 5.2 %collective-permute-start.6 = (f32[8,128]{1,0:T(8,128)S(1)}, f32[8,128]{1,0:T(8,128)S(1)}, u32[]{:S(2)}, u32[]{:S(2)}) collective-permute-start(f32[8,128]{1,0:T(8,128)S(1)} %fusion.8), channel_id=1, source_target_pairs={{128,0},{144,16},{160,32},{176,48},{192,64},{208,80},{224,96},{240... | collective-permute-start | bytes 12296 | tf_op jit(solution)/shard_map/ppermute | solution.py:25
Sparse Core Ops, SparseCore 0:
  16.6 152.6 all-reduce.3
where the time goes:
time: 374 us; the launch traced here: 371 us
  waiting for transfers between devices  151 us (40%)
  blocking collectives  129 us (34%)
  local copies, waits for them, and re-layouts  44 us (12%)
  between operations  21.1 us (6%)
  starting transfers between devices  10.2 us (3%)
  other arithmetic  8.6 us (2%)
  matrix products  7.55 us (2%)
    psum x1, waiting for transfers between devices, local(): lax.psum((jnp.dot(hidden, w_query, preferred_element_type=jnp.float32), j...  137 us
    all_gather x2, blocking collectives, local(): gathered = lax.all_gather(own_piece, 'pair', axis=0, tiled=True)  77.7 us
    psum x1, blocking collectives, local(): results.append(lax.psum(projected, 'tp'))  51.3 us
    scatter x2, local copies, waits for them, and re-layouts, local(): kv_store.at[targets]  14.3 us
    ppermute x2, waiting for transfers between devices, from_behind(): return lax.ppermute(block, axis, route)  8.06 us
    ppermute x6, starting transfers between devices, from_behind_2(): return lax.ppermute(block, axis, route)  7.57 us
  transfers between devices with their start and end apart: 9, of which 4 were waited for; matrix products, arithmetic and copies ran while one was open for 6% of the time, Pallas kernels for 0%

commit v1 on v0

v1 whole, which is shorter than its diff:
```python
import functools
import math

import jax
import jax.numpy as jnp
import numpy as np
from jax import lax
from jax.experimental import pallas as pl
from jax.experimental.pallas import tpu as pltpu
from jax.sharding import PartitionSpec as P

MESH = pl.DeviceIdType.MESH
PAGES_HALF = 384
SECTION = 64
STEPS = 2
BASE = 1000000.0
LANES = 128
RING = 4
NEW_ROWS = 8
CHUNK = 64


def sin_cos(angle):
    turns = jnp.floor(angle * (2.0 / math.pi) + 0.5)
    rest = angle - turns * 1.5703125
    rest = rest - turns * 4.837512969970703125e-4
    rest = rest - turns * 7.54978995489188216e-8
    sq = rest * rest
    sine = rest + rest * sq * (
        -1.6666654611e-1 + sq * (8.3321608736e-3 + sq * -1.9515295891e-4)
    )
    cosine = (
        1.0
        - 0.5 * sq
        + sq * sq * (4.166664568298827e-2 + sq * (-1.388731625493765e-3 + sq * 2.443315711809948e-5))
    )
    quarter = turns - 4.0 * jnp.floor(turns * 0.25)
    swap = (quarter == 1.0) | (quarter == 3.0)
    sine_out = jnp.where(swap, cosine, sine)
    cosine_out = jnp.where(swap, sine, cosine)
    sine_out = jnp.where(quarter >= 2.0, -sine_out, sine_out)
    cosine_out = jnp.where((quarter == 1.0) | (quarter == 2.0), -cosine_out, cosine_out)
    return sine_out, cosine_out


def attend_kernel(
    pair_count,
    tp_count,
    normed,
    w_query,
    b_query,
    w_key,
    b_key,
    w_value,
    b_value,
    w_out,
    pool,
    table,
    lengths,
    freq,
    attended,
    incoming,
    fresh,
    pages,
    hidden_v,
    bias_q,
    bias_k,
    bias_v,
    table_s,
    table_v,
    length_s,
    freq_v,
    wq,
    wk,
    wv,
    wo,
    outgoing,
    passing,
    part,
    parts,
    scores,
    bias,
    half,
    halves,
    merged,
    proj,
    projs,
    load_sem,
    s1,
    r1,
    s1_new,
    r1_new,
    s2,
    r2,
    s3,
    r3,
    sm,
    rm,
    rp,
    sf,
    ready,
):
    requests = pair_count // 2
    me = lax.axis_index("pair")
    tp = lax.axis_index("tp")
    request = lax.rem(me, requests)
    source = me >= requests
    pair_peers = [lax.rem(me + d, pair_count) for d in range(1, pair_count)]
    tp_peers = [lax.rem(tp + d, tp_count) for d in range(1, tp_count)]

    far = lax.rem(tp, 2)
    near_peers = [lax.rem(tp + d, tp_count) for d in range(2, tp_count, 2)]
    far_peers = [lax.rem(tp + d, tp_count) for d in range(1, tp_count, 2)]
    barrier = pltpu.get_barrier_semaphore()
    for q in pair_peers:
        pl.semaphore_signal(barrier, inc=1, device_id={"pair": q}, device_id_type=MESH)
    for q in near_peers:
        pl.semaphore_signal(barrier, inc=1, device_id={"tp": q}, device_id_type=MESH)

    @pl.when(far == 0)
    def _():
        for q in far_peers:
            pl.semaphore_signal(barrier, inc=1, device_id={"tp": q}, device_id_type=MESH)

    operands = (
        (normed, hidden_v),
        (w_query, wq),
        (w_key, wk),
        (w_value, wv),
        (table, table_s),
        (pool.at[0, 0], pages),
        (table, table_v),
        (lengths, length_s),
        (freq, freq_v),
        (b_query, bias_q),
        (b_key, bias_k),
        (b_value, bias_v),
        (w_out, wo),
    )
    loads = [
        pltpu.make_async_copy(here, there, load_sem.at[i])
        for i, (here, there) in enumerate(operands)
    ]
    for load in loads:
        load.start()

    part[...] = jnp.zeros(part.shape, part.dtype)
    heads = wq.shape[1] // LANES
    loads[0].wait()
    hidden = hidden_v[...].reshape(STEPS * requests, hidden_v.shape[2])
    loads[1].wait()
    query = jnp.dot(hidden, wq[...], preferred_element_type=jnp.float32)
    for s in range(STEPS):
        for h in range(heads):
            part[:, s * heads + h, :] = query[
                s * requests : (s + 1) * requests, h * LANES : (h + 1) * LANES
            ]
    loads[2].wait()
    loads[3].wait()
    key = jnp.dot(hidden, wk[...], preferred_element_type=jnp.float32)
    value = jnp.dot(hidden, wv[...], preferred_element_type=jnp.float32)
    count = STEPS * heads
    for s in range(STEPS):
        part[:, count + s, :] = key[s * requests : (s + 1) * requests]
        part[:, count + STEPS + s, :] = value[s * requests : (s + 1) * requests]

    loads[4].wait()
    loads[5].wait()

    @pl.when(source)
    def _():
        for i in range(STEPS * SECTION):
            outgoing[i] = pages[table_s[0, i]]

    pl.semaphore_wait(barrier, pair_count - 1 + len(near_peers) + far * len(far_peers))

    @pl.when(far == 1)
    def _():
        for q in far_peers:
            pl.semaphore_signal(ready, inc=1, device_id={"tp": q}, device_id_type=MESH)

    first = []
    first_new = []
    for d in range(1, pair_count):
        peer = pair_peers[d - 1]
        at = lax.rem(peer, requests)
        copy = pltpu.make_async_remote_copy(
            src_ref=part.at[at, pl.ds(0, count)],
            dst_ref=parts.at[me, pl.ds(0, count)],
            send_sem=s1.at[d - 1],
            recv_sem=r1.at[d - 1],
            device_id={"pair": peer},
            device_id_type=MESH,
        )
        copy.start()
        first.append(copy)
        copy = pltpu.make_async_remote_copy(
            src_ref=part.at[at, pl.ds(count, NEW_ROWS)],
            dst_ref=parts.at[me, pl.ds(count, NEW_ROWS)],
            send_sem=s1_new.at[d - 1],
            recv_sem=r1_new.at[d - 1],
            device_id={"pair": peer},
            device_id_type=MESH,
        )

        @pl.when(peer >= requests)
        def _():
            copy.start()

        first_new.append(copy)

    column = pair_count // RING
    up, down = lax.rem(me + column, pair_count), lax.rem(me + pair_count - column, pair_count)
    section = outgoing.shape[0] // 2
    moves = [
        pltpu.make_async_remote_copy(
            src_ref=outgoing.at[pl.ds(i * section, section)],
            dst_ref=passing,
            send_sem=sm.at[i],
            recv_sem=rp,
            device_id={"pair": way},
            device_id_type=MESH,
        )
        for i, way in enumerate((up, down))
    ]

    @pl.when(source)
    def _():
        for move in moves:
            move.start()

    parts[me] = part[request]

    for load in loads[6:12]:
        load.wait()
    length = length_s[request]
    half_tokens = PAGES_HALF * pages.shape[1]
    limit = jnp.where(source, length - half_tokens, half_tokens)
    slots = pages.shape[0]
    page_len = pages.shape[1]
    per_row = LANES // page_len
    order = table_v[...]
    start = lax.broadcasted_iota(jnp.int32, (1, slots), 1) * page_len
    kept = jnp.clip(limit - start, 0, page_len).astype(jnp.float32)
    row_of = lax.broadcasted_iota(jnp.int32, (slots // per_row, slots), 0)
    lane_of = lax.broadcasted_iota(jnp.int32, (LANES, slots), 0)
    hit_row = jnp.where((order // per_row) == row_of, 1.0, 0.0).astype(jnp.bfloat16)
    hit_lane = jnp.where((order % per_row) == (lane_of // page_len), kept, 0.0).astype(jnp.bfloat16)
    seen = lax.dot_general(
        hit_row, hit_lane, (((1,), (1,)), ((), ())), preferred_element_type=jnp.float32
    )
    lane = lax.broadcasted_iota(jnp.int32, seen.shape, 1)
    bias[...] = jnp.where((lane % page_len).astype(jnp.float32) < seen, 0.0, -1e30)

    row = lax.broadcasted_iota(jnp.int32, (count + NEW_ROWS, LANES), 0)
    step = jnp.where(row < count, row // heads, row - count)
    angle = (length + step).astype(jnp.float32) * freq_v[...]
    sine, cosine = sin_cos(angle)
    lane = lax.broadcasted_iota(jnp.int32, (count + NEW_ROWS, LANES), 1)
    sine = jnp.where(lane < LANES // 2, -sine, sine)
    turned = row < count + STEPS
    query_bias = bias_q[...].reshape(heads, LANES)
    key_bias = bias_k[...].reshape(1, LANES)
    value_bias = bias_v[...].reshape(1, LANES)
    rest = row[count:]
    add = jnp.concatenate(
        [query_bias] * STEPS
        + [
            jnp.where(
                rest < count + STEPS,
                key_bias,
                jnp.where(rest < count + 2 * STEPS, value_bias, 0.0),
            )
        ],
        0,
    )

    for d in range(1, pair_count):
        first[d - 1].wait()

        @pl.when(pair_peers[d - 1] >= requests)
        def _():
            first_new[d - 1].wait_send()

    @pl.when(source)
    def _():
        for copy in first_new:
            copy.wait_recv()

    total = add
    for p in range(pair_count):
        total = total + parts[p]
    rotated = total * cosine + pltpu.roll(total, LANES // 2, 1) * sine
    total = jnp.where(turned, rotated, total)
    queries = total[:count].astype(jnp.bfloat16)
    new = jnp.where(source, total[count:], 0.0)
    fresh[...] = new
    new_rows = new.astype(jnp.bfloat16)
    new_values = pltpu.roll(new, NEW_ROWS - STEPS, 0).astype(jnp.bfloat16)

    scale = 1.0 / math.sqrt(LANES)
    contract_last = (((1,), (1,)), ((), ()))
    own = lax.dot_general(queries, new_rows, contract_last, preferred_element_type=jnp.float32)
    own = own * scale
    token = lax.broadcasted_iota(jnp.int32, own.shape, 1)
    own_step = lax.broadcasted_iota(jnp.int32, own.shape, 0) // heads
    own_seen = (token <= own_step) & (token < jnp.where(source, STEPS, 0))
    own = jnp.where(own_seen, own, -1e30)

    chunk_tokens = CHUNK * page_len
    chunks = slots // CHUNK
    tiles = chunk_tokens // LANES
    highest = jnp.full((count, LANES), -1e30, jnp.float32)
    for c in range(chunks):
        keys = pages[pl.ds(c * CHUNK, CHUNK), :, pl.ds(0, LANES)].reshape(chunk_tokens, LANES)
        score = lax.dot_general(queries, keys, contract_last, preferred_element_type=jnp.float32)
        for t in range(tiles):
            tile = score[:, t * LANES : (t + 1) * LANES] * scale + bias[pl.ds(c * tiles + t, 1), :]
            scores[c * tiles + t] = tile
            highest = jnp.maximum(highest, tile)
    top = jnp.maximum(jnp.max(highest, 1, keepdims=True), jnp.max(own, 1, keepdims=True))
    own_weight = jnp.where(own_seen, jnp.exp(own - top), 0.0)
    sums = jnp.zeros((count, LANES), jnp.float32)
    out = jnp.dot(
        own_weight.astype(jnp.bfloat16), new_values, preferred_element_type=jnp.float32
    )
    for c in range(chunks):
        weights = []
        for t in range(tiles):
            weight = jnp.exp(scores[c * tiles + t] - top)
            sums = sums + weight
            weights.append(weight.astype(jnp.bfloat16))
        values = pages[pl.ds(c * CHUNK, CHUNK), :, pl.ds(LANES, LANES)].reshape(chunk_tokens, LANES)
        out = out + jnp.dot(
            jnp.concatenate(weights, 1), values, preferred_element_type=jnp.float32
        )
    mass = jnp.sum(sums, 1, keepdims=True) + jnp.sum(own_weight, 1, keepdims=True)

    half[pl.ds(0, count), :] = (out / mass).astype(jnp.bfloat16)
    lane = lax.broadcasted_iota(jnp.int32, (count, LANES), 1)
    stats = jnp.where(lane < 3, top, jnp.where(lane < 6, mass, 0.0))
    high = stats.astype(jnp.bfloat16).astype(jnp.float32)
    middle = (stats - high).astype(jnp.bfloat16).astype(jnp.float32)
    low = stats - high - middle
    addend = lane % 3
    stats = jnp.where(addend == 0, high, jnp.where(addend == 1, middle, low))
    half[pl.ds(count, count), :] = stats.astype(jnp.bfloat16)

    second = []
    for d in range(1, pair_count):
        copy = pltpu.make_async_remote_copy(
            src_ref=half,
            dst_ref=halves.at[me],
            send_sem=s2.at[d - 1],
            recv_sem=r2.at[d - 1],
            device_id={"pair": pair_peers[d - 1]},
            device_id_type=MESH,
        )
        copy.start()
        second.append(copy)

    upward = (me < column) | (me >= pair_count - column)
    forward = pltpu.make_async_remote_copy(
        src_ref=passing,
        dst_ref=incoming.at[pl.ds(jnp.where(upward, 0, section), section)],
        send_sem=sf,
        recv_sem=rm.at[jnp.where(upward, 0, 1)],
        device_id={"pair": jnp.where(upward, up, down)},
        device_id_type=MESH,
    )
    moves[0].wait_recv()
    forward.start()

    halves[me] = half[...]
    loads[12].wait()
    pick_row = lax.broadcasted_iota(jnp.int32, (LANES, 2 * LANES), 0)
    pick_lane = lax.broadcasted_iota(jnp.int32, (LANES, 2 * LANES), 1)
    pick = (pick_row < 6) & ((pick_row // 3) == (pick_lane // LANES))
    pick = jnp.where(pick, 1.0, 0.0).astype(jnp.bfloat16)
    for copy in second:
        copy.wait()

    many = requests * count

    def side(at):
        block = halves[pl.ds(at, requests)]
        result = block[:, :count].reshape(many, LANES).astype(jnp.float32)
        stat = jnp.dot(
            block[:, count:].reshape(many, LANES), pick, preferred_element_type=jnp.float32
        )
        return result, stat[:, :LANES], stat[:, LANES:]

    out_a, top_a, mass_a = side(0)
    out_b, top_b, mass_b = side(requests)
    joint = jnp.maximum(top_a, top_b)
    weight_a = mass_a * jnp.exp(top_a - joint)
    weight_b = mass_b * jnp.exp(top_b - joint)
    head_out = (weight_a * out_a + weight_b * out_b) / (weight_a + weight_b)
    merged[...] = head_out.reshape(requests, count, LANES)
    blocks = []
    for h in range(heads):
        blocks.append(
            jnp.concatenate([merged[:, s * heads + h, :] for s in range(STEPS)], 0)
        )
    attended_rows = jnp.concatenate(blocks, 1).astype(jnp.bfloat16)
    proj[...] = jnp.dot(
        attended_rows, wo[...], preferred_element_type=jnp.float32
    ).astype(jnp.bfloat16)

    @pl.when(far == 0)
    def _():
        pl.semaphore_wait(ready, len(far_peers))

    third = []
    for d in range(1, tp_count):
        copy = pltpu.make_async_remote_copy(
            src_ref=proj,
            dst_ref=projs.at[tp],
            send_sem=s3.at[d - 1],
            recv_sem=r3.at[d - 1],
            device_id={"tp": tp_peers[d - 1]},
            device_id_type=MESH,
        )
        copy.start()
        third.append(copy)
    projs[tp] = proj[...]
    for copy in third:
        copy.wait()
    result = projs[0].astype(jnp.float32)
    for t in range(1, tp_count):
        result = result + projs[t].astype(jnp.float32)
    attended[...] = result.reshape(attended.shape)

    @pl.when(source)
    def _():
        for move in moves:
            move.wait_send()

    forward.wait_send()

    @pl.when(jnp.logical_not(source))
    def _():
        for i in range(2):
            pltpu.make_async_remote_copy(
                src_ref=passing,
                dst_ref=incoming.at[pl.ds(i * section, section)],
                send_sem=sf,
                recv_sem=rm.at[i],
                device_id={"pair": up},
                device_id_type=MESH,
            ).wait_recv()


def pool_kernel(
    requests,
    base,
    incoming,
    fresh,
    result,
    table,
    lengths,
    plan,
    attended,
    new_pool,
    pages,
    table_s,
    length_s,
    plan_s,
    load_sem,
    store_sem,
):
    del base
    me = lax.axis_index("pair")
    request = lax.rem(me, requests)
    source = me >= requests
    page_len = pages.shape[1]
    operands = ((table, table_s), (lengths, length_s), (plan, plan_s))
    loads = [
        pltpu.make_async_copy(here, there, load_sem.at[i])
        for i, (here, there) in enumerate(operands)
    ]
    for load in loads:
        load.start()
    store_result = pltpu.make_async_copy(result, attended, store_sem.at[0])
    store_result.start()
    for load in loads:
        load.wait()

    @pl.when(jnp.logical_not(source))
    def _():
        handed = plan_s[0, request] + plan_s[1, request]

        def put(i, carry):
            pages[table_s[0, PAGES_HALF + i]] = incoming[i]
            return carry

        lax.fori_loop(0, handed, put, 0)

    @pl.when(source)
    def _():
        for s in range(STEPS):
            offset = length_s[request] - PAGES_HALF * page_len + s
            slot = table_s[0, offset // page_len]
            line = offset % page_len
            entry = jnp.concatenate([fresh[pl.ds(s, 1), :], fresh[pl.ds(STEPS + s, 1), :]], 1)
            old = pages[slot].astype(jnp.float32)
            at = lax.broadcasted_iota(jnp.int32, old.shape, 0)
            pages[slot] = jnp.where(at == line, entry, old).astype(pages.dtype)

    store = pltpu.make_async_copy(pages, new_pool.at[0, 0], store_sem.at[1])
    store.start()
    store_result.wait()
    store.wait()


def local(
    normed, w_query, b_query, w_key, b_key, w_value, b_value, w_out, pool, page_table, lengths, plan
):
    pair_count = lax.axis_size("pair")
    tp_count = lax.axis_size("tp")
    requests = pair_count // 2
    head_size = w_key.shape[1]
    heads = w_query.shape[1] // head_size
    count = STEPS * heads
    slots, page_len, width = pool.shape[2:]
    moved = STEPS * SECTION
    model = w_query.shape[0]
    out_width = w_out.shape[1]
    half_index = np.arange(head_size) % (head_size // 2)
    freq = jnp.asarray(
        (BASE ** (-(half_index * 2.0 / head_size))).astype(np.float32)[None, :]
    )
    bf16, f32 = jnp.bfloat16, jnp.float32
    vmem = pl.BlockSpec(memory_space=pltpu.VMEM)
    hbm = pl.BlockSpec(memory_space=pltpu.HBM)
    dma = pltpu.SemaphoreType.DMA
    regular = pltpu.SemaphoreType.REGULAR
    others = pair_count - 1
    keep = functools.partial(pltpu.with_memory_space_constraint, memory_space=pltpu.HBM)
    near = functools.partial(pltpu.with_memory_space_constraint, memory_space=pltpu.VMEM)
    operands = (
        normed, w_query, b_query, w_key, b_key, w_value, b_value, w_out, pool,
        page_table, lengths, freq,
    )
    attended, incoming, fresh, pages = pl.pallas_call(
        functools.partial(attend_kernel, pair_count, tp_count),
        name="attend",
        out_shape=(
            pltpu.VMEM(normed.shape[:2] + (out_width,), f32),
            pltpu.VMEM((moved, page_len, width), bf16),
            pltpu.VMEM((NEW_ROWS, head_size), f32),
            pltpu.VMEM((slots, page_len, width), bf16),
        ),
        in_specs=[hbm] * len(operands),
        out_specs=(vmem,) * 4,
        scratch_shapes=[
            pltpu.VMEM(normed.shape, bf16),
            pltpu.VMEM(b_query.shape, f32),
            pltpu.VMEM(b_key.shape, f32),
            pltpu.VMEM(b_value.shape, f32),
            pltpu.SMEM(page_table.shape, jnp.int32),
            pltpu.VMEM(page_table.shape, jnp.int32),
            pltpu.SMEM(lengths.shape, jnp.int32),
            pltpu.VMEM(freq.shape, f32),
            pltpu.VMEM((model, heads * head_size), bf16),
            pltpu.VMEM((model, head_size), bf16),
            pltpu.VMEM((model, head_size), bf16),
            pltpu.VMEM((heads * head_size, out_width), bf16),
            pltpu.VMEM((moved, page_len, width), bf16),
            pltpu.VMEM((moved // 2, page_len, width), bf16),
            pltpu.VMEM((requests, count + NEW_ROWS, head_size), f32),
            pltpu.VMEM((pair_count, count + NEW_ROWS, head_size), f32),
            pltpu.VMEM((slots * page_len // LANES, count, LANES), f32),
            pltpu.VMEM((slots * page_len // LANES, LANES), f32),
            pltpu.VMEM((2 * count, head_size), bf16),
            pltpu.VMEM((pair_count, 2 * count, head_size), bf16),
            pltpu.VMEM((requests, count, head_size), f32),
            pltpu.VMEM((STEPS * requests, out_width), bf16),
            pltpu.VMEM((tp_count, STEPS * requests, out_width), bf16),
            dma((13,)),
            dma((others,)),
            dma((others,)),
            dma((others,)),
            dma((others,)),
            dma((others,)),
            dma((others,)),
            dma((tp_count - 1,)),
            dma((tp_count - 1,)),
            dma((2,)),
            dma((2,)),
            dma,
            dma,
            regular,
        ],
        compiler_params=pltpu.CompilerParams(
            collective_id=0, has_side_effects=True, vmem_limit_bytes=28 * 2**20
        ),
    )(*(keep(x) for x in operands))
    attended, new_pool, _ = pl.pallas_call(
        functools.partial(pool_kernel, requests),
        name="place",
        out_shape=(
            pltpu.HBM(attended.shape, f32),
            pltpu.HBM(pool.shape, bf16),
            pltpu.VMEM(pages.shape, bf16),
        ),
        in_specs=[vmem] * 7,
        out_specs=(hbm, hbm, vmem),
        input_output_aliases={0: 2},
        scratch_shapes=[
            pltpu.SMEM(page_table.shape, jnp.int32),
            pltpu.SMEM(lengths.shape, jnp.int32),
            pltpu.SMEM(plan.shape[::-1], jnp.int32),
            dma((3,)),
            dma((2,)),
        ],
        compiler_params=pltpu.CompilerParams(vmem_limit_bytes=8 * 2**20),
    )(*(near(x) for x in (pages, incoming, fresh, attended, page_table, lengths, plan.T)))
    return attended, new_pool


def solution(mesh):
    return jax.shard_map(
        local,
        mesh=mesh,
        in_specs=(
            P(None, "rep", "pair"),
            P("pair", "tp"),
            P("tp"),
            P("pair", "tp"),
            P("tp"),
            P("pair", "tp"),
            P("tp"),
            P("tp", "pair"),
            P(("rep", "pair"), "tp", None, None, None),
            P(("rep", "pair"), None),
            P("rep"),
            P("rep", None),
        ),
        out_specs=(P(None, "rep", "pair"), P(("rep", "pair"), "tp", None, None, None)),
        check_vma=False,
    )
```

time: 374 us -> 40 us (0.11)
  waiting for transfers between devices: 151 us -> 0 us
  blocking collectives: 129 us -> 0 us
  local copies, waits for them, and re-layouts: 44 us -> 0.01 us
  Pallas kernels: 0 us -> 39.2 us
  between operations: 21.1 us -> 0.69 us
  starting transfers between devices: 10.2 us -> 0 us
  other arithmetic: 8.6 us -> 0 us
  matrix products: 7.55 us -> 0 us
    psum x1 -> x0, waiting for transfers between devices: 137 us -> none  [local(): lax.psum((jnp.dot(hidden, w_query, preferred_element_type=jnp.float32), j...]
    all_gather x2 -> x0, blocking collectives: 77.7 us -> none  [local(): gathered = lax.all_gather(own_piece, 'pair', axis=0, tiled=True)]
    psum x1 -> x0, blocking collectives: 51.3 us -> none  [local(): results.append(lax.psum(projected, 'tp'))]
    pallas_call x0 -> x2, Pallas kernels: none -> 39.2 us  [the longest x1 36.2 us: local(): pl.pallas_call(functools.partial(attend_kernel, pair_count, tp_count), na...]
    gather x8 -> x0, local copies, waits for them, and re-layouts: 14.3 us -> none  [the longest x4 7.15 us: local(): outgoing = kv_store[slot_table[page_picks]]]
    scatter x2 -> x0, local copies, waits for them, and re-layouts: 14.3 us -> none  [local(): kv_store.at[targets]]
    ppermute x8 -> x0, waiting for transfers between devices: 13.2 us -> none  [the longest x2 8.06 us: from_behind(): return lax.ppermute(block, axis, route)]
    ppermute x8 -> x0, starting transfers between devices: 10.2 us -> none  [the longest x6 7.57 us: from_behind_2(): return lax.ppermute(block, axis, route)]
  transfers between devices with their start and end apart: 9 -> 0, of which waited for: 4 -> 0; matrix products, arithmetic and copies ran while one was open for 6% -> 0% of each run, Pallas kernels for 0% -> 0%
where the time goes in v1:
time: 40 us; the launch traced here: 39.9 us
  Pallas kernels  39.2 us (98%)
  between operations  0.69 us (2%)
    pallas_call x1, Pallas kernels, local(): pl.pallas_call(functools.partial(attend_kernel, pair_count, tp_count), na...  36.2 us
    pallas_call x1, Pallas kernels, local(): pl.pallas_call(functools.partial(pool_kernel, requests), name='place', ou...  3.01 us

profile of v1, /device:TPU:8, one launch (start us, length us, event | category | flops | bytes accessed | tf_op | source)
XLA Modules:
  0.0 39.9 jit_solution(7867313563394806877)
XLA Ops:
  0.6 0.0 copy-start.1
  0.6 0.0 copy-start
  0.7 0.0 copy-start.2
  0.7 36.2 %attend.1 = (f32[2,8,512]{2,1,0:T(8,128)S(1)}, bf16[128,16,256]{2,1,0:T(8,128)(2,1)S(1)}, f32[8,128]{1,0:T(8,128)S(1)}, bf16[512,16,256]{2,1,0:T(8,128)(2,1)S(1)}) custom-call(bf16[2,8,512]{2,1,0:T(8,128)(2,1)} %normed.1, bf16[512,1024]{1,0:T(8,128)(2,1)} %w_query.1, f32[1024]{0:T(1024)} %b_query.1, bf16[512,128]{1,0:T(8,128)(2,1)} %w_key.1, f32[128]{0:T(128)} %b_key.1, ...), custom_call_target="tpu_custom_call" | custom-call | tf_op jit(solution)/shard_map/attend/pallas_call | solution.py:545
  36.8 0.0 copy-done.1
  36.8 0.0 copy-done
  36.9 0.0 copy-done.2
  36.9 3.0 %place.1 = (f32[2,8,512]{2,1,0:T(8,128)}, bf16[1,1,512,16,256]{4,3,2,1,0:T(8,128)(2,1)}, bf16[512,16,256]{2,1,0:T(8,128)(2,1)S(1)}) custom-call(bf16[512,16,256]{2,1,0:T(8,128)(2,1)S(1)} %get-tuple-element.8.base, bf16[128,16,256]{2,1,0:T(8,128)(2,1)S(1)} %get-tuple-element.9.incoming, ...), custom_call_target="tpu_custom_call", output_to_operand_aliasing={{2}: (0, {})} | custom-call | tf_op jit(solution)/shard_map/place/pallas_call | solution.py:599
Async XLA Ops:
  0.6 36.2 %copy-start.1 = (s32[8]{0:T(128)S(1)}, s32[8]{0:T(128)}, u32[]{:S(2)}) copy-start(s32[8]{0:T(128)} %lengths.3) | copy-start | bytes 100
  0.6 36.2 %copy-start = (s32[1,512]{1,0:T(1,128)S(1)}, s32[1,512]{1,0:T(1,128)}, u32[]{:S(2)}) copy-start(s32[1,512]{1,0:T(1,128)} %table.3) | copy-start | bytes 6148
  0.7 36.2 %copy-start.2 = (s32[8,2]{0,1:T(2,128)S(1)}, s32[8,2]{0,1:T(2,128)}, u32[]{:S(2)}) copy-start(s32[8,2]{0,1:T(2,128)} %param.24) | copy-start | bytes 196
